TPU v7x, 256 devices: a whole 4x4x8 slice. The times are simulated.
256 devices in a mesh: branch: 32 (over y, z), tensor: 8 (over x, core).
Axes of the slice: x: 4, y: 4, z: 8, core: 2. Of those that a mesh axis runs over, the one named last changes fastest.
Arguments:
- query: bfloat16 [256, 2, 128, 192], P('branch', None, 'tensor'), may hold values from -52 to 52
- absorb_key: bfloat16 [128, 128, 512], P('tensor'), may hold values from -0.5 to 0.5
- absorb_value: bfloat16 [128, 512, 128], P('tensor'), may hold values from -0.25 to 0.25
- prefix_cache: bfloat16 [2048, 576], replicated, may hold values from -6 to 6
- home_cache: bfloat16 [256, 256, 576], P('branch'), may hold values from -6 to 6
- spill_pool: bfloat16 [1024, 128, 576], P('branch'), may hold values from -6 to 6
- new_latent: bfloat16 [256, 2, 576], P('branch', None, 'tensor'), may hold values from -6 to 6
- lengths: int32 [256], P('branch'), may hold values from 1 to 768, as said below
- spill_table: int32 [256, 4], P('branch'), may hold values from 0 to 1023, as said below
Outputs:
- head_output: bfloat16 [256, 2, 128, 128], P('branch', None, 'tensor')
Inputs may be any that keep to these rules, and one draw needn't show every extreme that they name: Every branch has at least one cached suffix token; in every draw some branch has exactly 768. Branch b lies on device d = b // 8 of branch, and its k-th spilled block (for k * 128 < lengths[b] - 256) sits in pool slot h * 32 + d + c of some holder device h and some c < 1; distinct blocks have distinct slots. `spill_table`: entries of blocks beyond a branch's length are valid slot numbers that carry nothing.
All inputs are finite; a program needn't handle non-finite values.
Results may differ from a plain program's by a relative error of at most 0.012.
The roundings to bfloat16 on the way count: a program that leaves them out, or rounds other values in their place, can miss the bound.
Values may be sent and summed in bfloat16 or wider, within the bound.
A program may use at most 64 MiB of HBM per device.

v0:
```python
import jax
import jax.numpy as jnp
from jax import lax
from jax.sharding import PartitionSpec as P

floor_value = -1e30


def masked_part(scores, valid):
    row_peak = jnp.max(jnp.where(valid, scores, floor_value), -1)
    weights = jnp.where(valid, jnp.exp(scores - row_peak[..., None]), 0.0)
    row_mass = jnp.sum(weights, -1)
    return (row_peak, row_mass, weights.astype(jnp.bfloat16))


def per_device(
    query,
    absorb_key,
    absorb_value,
    prefix_cache,
    home_cache,
    spill_pool,
    new_latent,
    lengths,
    spill_table,
):
    branch_count, step_count, head_count, query_width = query.shape
    nope_width = absorb_key.shape[1]
    latent_width = absorb_key.shape[2]
    home_len = home_cache.shape[1]
    block_len = spill_pool.shape[1]
    key_width = prefix_cache.shape[1]
    dev_count = lax.axis_size("branch")
    slot_count = spill_pool.shape[0]
    slot_cap = slot_count // dev_count
    per_branch = spill_table.shape[1]
    score_scale = query_width ** (-0.5)
    row_count = step_count * head_count
    fresh = lax.all_gather(new_latent, "tensor", axis=2, tiled=True)
    latent_query = jnp.einsum(
        "bshn,hnl->bshl", query[..., :nope_width], absorb_key, preferred_element_type=jnp.float32
    ).astype(jnp.bfloat16)
    full_query = jnp.concatenate([latent_query, query[..., nope_width:]], -1).reshape(
        branch_count, row_count, key_width
    )
    partials = []
    prefix_scores = (
        jnp.einsum("brk,tk->brt", full_query, prefix_cache, preferred_element_type=jnp.float32)
        * score_scale
    )
    row_peak, row_mass, weights = masked_part(prefix_scores, True)
    partials.append(
        (
            row_peak,
            row_mass,
            jnp.einsum(
                "brt,tl->brl",
                weights,
                prefix_cache[:, :latent_width],
                preferred_element_type=jnp.float32,
            ),
        )
    )
    home_valid = (jnp.arange(home_len)[None, :] < lengths[:, None])[:, None, :]
    home_scores = (
        jnp.einsum("brk,btk->brt", full_query, home_cache, preferred_element_type=jnp.float32)
        * score_scale
    )
    row_peak, row_mass, weights = masked_part(home_scores, home_valid)
    partials.append(
        (
            row_peak,
            row_mass,
            jnp.einsum(
                "brt,btl->brl",
                weights,
                home_cache[..., :latent_width],
                preferred_element_type=jnp.float32,
            ),
        )
    )
    step_of_row = jnp.arange(row_count) // head_count
    fresh_valid = (jnp.arange(step_count)[None, :] <= step_of_row[:, None])[None]
    fresh_scores = (
        jnp.einsum("brk,bjk->brj", full_query, fresh, preferred_element_type=jnp.float32)
        * score_scale
    )
    row_peak, row_mass, weights = masked_part(fresh_scores, fresh_valid)
    partials.append(
        (
            row_peak,
            row_mass,
            jnp.einsum(
                "brj,bjl->brl",
                weights,
                fresh[..., :latent_width],
                preferred_element_type=jnp.float32,
            ),
        )
    )
    spill_offset = lengths - home_len
    slot_of_block = spill_table // slot_count * slot_cap + spill_table % slot_cap
    received = lax.all_to_all(
        spill_pool.reshape(dev_count, slot_cap, block_len, key_width),
        "branch",
        split_axis=0,
        concat_axis=0,
        tiled=True,
    )
    received = received.reshape(slot_count, block_len, key_width)
    gathered = jnp.take(received, slot_of_block.reshape(-1), axis=0).reshape(
        branch_count, per_branch * block_len, key_width
    )
    spill_valid = (jnp.arange(per_branch * block_len)[None, :] < spill_offset[:, None])[:, None, :]
    spill_scores = (
        jnp.einsum("brk,btk->brt", full_query, gathered, preferred_element_type=jnp.float32)
        * score_scale
    )
    row_peak, row_mass, weights = masked_part(spill_scores, spill_valid)
    partials.append(
        (
            row_peak,
            row_mass,
            jnp.einsum(
                "brt,btl->brl",
                weights,
                gathered[..., :latent_width],
                preferred_element_type=jnp.float32,
            ),
        )
    )
    best_peak = partials[0][0]
    for entry in partials[1:]:
        best_peak = jnp.maximum(best_peak, entry[0])
    mass_total = jnp.zeros_like(best_peak)
    sums_total = jnp.zeros(partials[0][2].shape, jnp.float32)
    for entry in partials:
        factor = jnp.exp(entry[0] - best_peak)
        mass_total = mass_total + entry[1] * factor
        sums_total = sums_total + entry[2] * factor[..., None]
    latent_out = (
        (sums_total / mass_total[..., None])
        .astype(jnp.bfloat16)
        .reshape(branch_count, step_count, head_count, latent_width)
    )
    head_output = jnp.einsum(
        "bshl,hlv->bshv", latent_out, absorb_value, preferred_element_type=jnp.float32
    )
    return head_output.astype(jnp.bfloat16)


def solution(mesh):
    in_specs = (
        P("branch", None, "tensor", None),
        P("tensor", None, None),
        P("tensor", None, None),
        P(),
        P("branch", None, None),
        P("branch", None, None),
        P("branch", None, "tensor"),
        P("branch"),
        P("branch", None),
    )
    out_specs = P("branch", None, "tensor", None)
    return jax.shard_map(
        per_device, mesh=mesh, in_specs=in_specs, out_specs=out_specs, check_vma=False
    )
```

profile of v0, /device:TPU:6, one launch (start us, length us, event | category | flops | bytes accessed | tf_op | source)
XLA Modules:
  0.0 145.7 jit_solution(8986966199239067726)
XLA Ops:
  0.0 11.7 %all-to-all-start = ((bf16[32,1,128,576]{2,3,1,0:T(8,128)(2,1)}), bf16[32,1,128,576]{2,3,1,0:T(8,128)(2,1)}, u32[]{:S(2)}, u32[]{:S(2)}) async-start(bf16[32,1,128,576]{2,3,1,0:T(8,128)(2,1)} %bitcast.54), calls=%async_computation | async-start | bytes 9437184 | tf_op jit(solution)/shard_map/all_to_all | solution.py:103
  12.0 0.4 fusion.33
  12.7 12.9 %all_gather.3 = bf16[8,2,576]{0,1,2:T(2,128)(2,1)S(1)} all-gather(bf16[8,2,72]{0,1,2:T(2,128)(2,1)S(1)} %copy.33), channel_id=1, replica_groups=mesh['branch'=32,'tensor'=8] {'tensor'}, dimensions={2}, use_global_device_ids=true | all-gather | bytes 20736 | tf_op jit(solution)/shard_map/all_gather | solution.py:39
  25.8 0.2 select_reduce_fusion.2
  26.1 2.4 %select_reduce_fusion.1 = (f32[8,32]{1,0:T(8,128)S(1)}, f32[8,32,256]{2,1,0:T(8,128)S(1)}) fusion(pred[8,256]{1,0:T(8,128)(4,1)S(1)} %iota_compare_fusion.1, bf16[8,32,576]{2,1,0:T(8,128)(2,1)S(1)} %bitcast.56, bf16[8,256,576]{1,2,0:T(8,128)(2,1)} %param.13), kind=kOutput, calls=%fused_computation.44 | convolution fusion | flops 75693824 | bytes 2919424 | tf_op jit(solution)/shard_map/brk,btk->brt/dot_general | solution.py:66
  28.5 0.2 fusion.51
  28.7 1.1 fusion.67
  29.8 1.3 copy-done.3
  31.1 0.4 fusion.12
  31.7 88.4 %all-to-all-done = bf16[32,1,128,576]{2,3,1,0:T(8,128)(2,1)} async-done(((bf16[32,1,128,576]{2,3,1,0:T(8,128)(2,1)}), bf16[32,1,128,576]{2,3,1,0:T(8,128)(2,1)}, u32[]{:S(2)}, u32[]{:S(2)}) %all-to-all-start) | async-done | bytes 4718624 | tf_op jit(solution)/shard_map/all_to_all | solution.py:103
  120.1 5.7 %gather_fusion = bf16[32,128,576]{1,2,0:T(8,128)(2,1)} fusion(bf16[32,128,576]{1,2,0:T(8,128)(2,1)} %bitcast.8, s32[1024]{0:T(1024)S(1)} %pad_clamp_fusion), kind=kCustom, calls=%fused_computation | custom fusion | bytes 9437312 | tf_op jit(solution)/shard_map/jit(_take)/gather | solution.py:111
  125.8 7.6 %copy.36 = bf16[32,128,576]{2,1,0:T(8,128)(2,1)} copy(bf16[32,128,576]{1,2,0:T(8,128)(2,1)} %gather_fusion) | data formatting | bytes 9437184 | tf_op jit(solution)/shard_map/jit(_take)/gather | solution.py:111
  133.4 3.7 %bitcast_select_fusion = bf16[8,512,576]{2,1,0:T(8,128)(2,1)S(1)} fusion(pred[8,512]{1,0:T(8,128)(4,1)S(1)} %broadcast_bitcast_fusion, bf16[8,512,576]{2,1,0:T(8,128)(2,1)} %bitcast.53), kind=kLoop, calls=%fused_computation.1 | loop fusion | flops 2359296 | bytes 9441280 | tf_op jit(solution)/shard_map/jit(_take)/select_n | solution.py:111
  137.2 1.7 %select_reduce_fusion = (f32[8,32]{1,0:T(8,128)S(1)}, f32[8,32,512]{2,1,0:T(8,128)S(1)}) fusion(pred[8,512]{1,0:T(8,128)(4,1)S(1)} %iota_compare_fusion, bf16[8,32,576]{2,1,0:T(8,128)(2,1)S(1)} %bitcast.58, bf16[8,512,576]{2,1,0:T(8,128)(2,1)S(1)} %bitcast_select_fusion), kind=kOutput, calls=%fused_computation.36 | convolution fusion | flops 151387904 | bytes 5542912 | tf_op jit(solution)/shard_map/brk,btk->brt/dot_general | solution.py:116
  138.9 0.2 fusion.44
  139.2 0.7 fusion.20
  139.9 0.9 fusion.26
  140.8 0.7 copy-done.4
  141.5 0.7 copy-done.9
  142.2 0.8 fusion.17
  143.0 0.3 fusion.29
  143.3 1.3 copy-done.2
  144.6 0.5 fusion.39
  145.0 0.7 copy.41
  (38 shorter events, 0.9 us)
Async XLA Ops:
  0.0 12.0 %copy-start = (bf16[16,128,512]{2,1,0:T(8,128)(2,1)S(1)}, bf16[16,128,512]{2,1,0:T(8,128)(2,1)}, u32[]{:S(2)}) copy-start(bf16[16,128,512]{2,1,0:T(8,128)(2,1)} %param.10) | copy-start | bytes 6291460
  0.0 11.8 %copy-start.6 = (s32[8,4]{0,1:T(4,128)S(1)}, s32[8,4]{0,1:T(4,128)}, u32[]{:S(2)}) copy-start(s32[8,4]{0,1:T(4,128)} %param.17) | copy-start | bytes 388
  0.0 12.0 %slice-start.1 = ((bf16[8,2,16,192]{3,2,1,0:T(8,128)(2,1)}), bf16[8,2,16,64]{3,2,1,0:T(8,128)(2,1)S(1)}, s32[]{:S(2)}) async-start(bf16[8,2,16,192]{3,2,1,0:T(8,128)(2,1)} %param.9), calls=%async_computation.2 | async-start | bytes 131072 | tf_op jit(solution)/shard_map/slice | solution.py:43
  0.0 12.0 %slice-start = ((bf16[8,2,16,192]{3,2,1,0:T(8,128)(2,1)}), bf16[8,2,16,128]{3,2,1,0:T(8,128)(2,1)S(1)}, s32[]{:S(2)}) async-start(bf16[8,2,16,192]{3,2,1,0:T(8,128)(2,1)} %param.9), calls=%async_computation.1 | async-start | bytes 131072 | tf_op jit(solution)/shard_map/slice | solution.py:41
  0.0 120.1 %all-to-all-start = ((bf16[32,1,128,576]{2,3,1,0:T(8,128)(2,1)}), bf16[32,1,128,576]{2,3,1,0:T(8,128)(2,1)}, u32[]{:S(2)}, u32[]{:S(2)}) async-start(bf16[32,1,128,576]{2,3,1,0:T(8,128)(2,1)} %bitcast.54), calls=%async_computation | async-start | bytes 9437184 | tf_op jit(solution)/shard_map/all_to_all | solution.py:103
  11.8 0.8 copy-start.5
  12.0 14.0 %copy-start.7 = (s32[8]{0:T(128)S(1)}, s32[8]{0:T(128)}, u32[]{:S(2)}) copy-start(s32[8]{0:T(128)} %param.16) | copy-start | bytes 100
  25.7 3.0 %copy-start.8 = (bf16[2048,576]{0,1:T(8,128)(2,1)S(1)}, bf16[2048,576]{0,1:T(8,128)(2,1)}, u32[]{:S(2)}) copy-start(bf16[2048,576]{0,1:T(8,128)(2,1)} %param.12) | copy-start | bytes 7077892
  29.8 1.3 copy-start.3
  137.1 2.0 %copy-start.1 = (bf16[8,256,576]{1,2,0:T(8,128)(2,1)S(1)}, bf16[8,256,576]{1,2,0:T(8,128)(2,1)}, u32[]{:S(2)}) copy-start(bf16[8,256,576]{1,2,0:T(8,128)(2,1)} %param.13) | copy-start | bytes 7077892
  139.9 1.6 %copy-start.4 = (f32[8,32,2048]{2,1,0:T(8,128)S(1)}, f32[8,32,2048]{2,1,0:T(8,128)}, u32[]{:S(2)}) copy-start(f32[8,32,2048]{2,1,0:T(8,128)} %copy-done.3) | copy-start | bytes 6291460
  139.9 2.3 %copy-start.9 = (bf16[2048,576]{0,1:T(8,128)(2,1)S(1)}, bf16[2048,576]{0,1:T(8,128)(2,1)}, u32[]{:S(2)}) copy-start(bf16[2048,576]{0,1:T(8,128)(2,1)} %param.12) | copy-start | bytes 7077892
  143.0 1.6 %copy-start.2 = (bf16[16,512,128]{2,1,0:T(8,128)(2,1)S(1)}, bf16[16,512,128]{2,1,0:T(8,128)(2,1)}, u32[]{:S(2)}) copy-start(bf16[16,512,128]{2,1,0:T(8,128)(2,1)} %param.11) | copy-start | bytes 6291460
where the time goes:
time: 146 us
  waiting for transfers between devices  88.4 us (61%)
  local copies, waits for them, and re-layouts  18.6 us (13%)
  blocking collectives  12.9 us (9%)
  starting transfers between devices  11.7 us (8%)
  matrix products  8.92 us (6%)
  other arithmetic  4.9 us (3%)
    all_to_all x1, waiting for transfers between devices, per_device(): lax.all_to_all(spill_pool.reshape(dev_count, slot_cap, block_len, key_wid...  88.4 us
    gather x2, local copies, waits for them, and re-layouts, per_device(): jnp.take(received, slot_of_block.reshape(-1), axis=0)  13.3 us
    all_gather x1, blocking collectives, per_device(): fresh = lax.all_gather(new_latent, 'tensor', axis=2, tiled=True)  12.9 us
    all_to_all x1, starting transfers between devices, per_device(): lax.all_to_all(spill_pool.reshape(dev_count, slot_cap, block_len, key_wid...  11.7 us
    unnamed x22, local copies, waits for them, and re-layouts  4.19 us
    select_n x2, other arithmetic, per_device(): jnp.take(received, slot_of_block.reshape(-1), axis=0)  3.75 us
  transfers between devices with their start and end apart: 1, of which 1 were waited for; matrix products, arithmetic and copies ran while one was open for 4% of the time, Pallas kernels for 0%

commit v1 on v0

v1 whole, which is shorter than its diff:
```python
import functools
import math

import jax
import jax.numpy as jnp
from jax import lax
from jax.experimental import pallas as pl
from jax.experimental.pallas import tpu as pltpu
from jax.sharding import PartitionSpec as P

MESH = pl.DeviceIdType.MESH
FLOOR = -1e30
KEY_TILE = 512


def nt_dot(a, b):
    return lax.dot_general(a, b, (((1,), (1,)), ((), ())), preferred_element_type=jnp.float32)


def attention_kernel(
    dims,
    query_ref,
    wk_ref,
    wv_ref,
    prefix_ref,
    home_ref,
    pool_ref,
    fresh_ref,
    len_ref,
    table_ref,
    out_ref,
    q_buf,
    wk_buf,
    wv_buf,
    prefix_buf,
    home_buf,
    new_buf,
    spill,
    flat_buf,
    lat_buf,
    full_send,
    full_recv,
    fresh_send,
    fresh_recv,
    peak_buf,
    mass_buf,
    acc_buf,
    lo_send,
    lo_recv,
    out_buf,
    local_sem,
    q_send_sem,
    q_recv_sem,
    f_send_sem,
    f_recv_sem,
    s_send_sem,
    s_recv_sem,
    x_send_sem,
    x_recv_sem,
    o_send_sem,
    o_recv_sem,
    *chunk_bufs,
):
    n_dev, n_ten, branches, steps, heads, nope, rope, latent, home, block, per_branch, chunks = dims
    width = latent + rope
    rows = steps * heads
    bs = branches * steps
    all_rows = n_ten * rows
    n_chunk = len(chunks)
    pair_rows = 2 * width // n_ten
    even_rows = sum(wide[0] for wide in chunks)
    pool_recv = chunk_bufs[:n_chunk]
    stage = chunk_bufs[n_chunk:]
    me = lax.axis_index("branch")
    mine = lax.axis_index("tensor")
    scale = (nope + rope) ** -0.5 / math.log(2.0)

    def dev(i):
        return lax.rem(me + i, n_dev)

    def ten(i):
        return lax.rem(mine + i, n_ten)

    barrier = pltpu.get_barrier_semaphore()

    def greet_dev(i, carry):
        pl.semaphore_signal(barrier, inc=1, device_id={"branch": dev(i)}, device_id_type=MESH)
        return carry

    def greet_ten(i, carry):
        pl.semaphore_signal(barrier, inc=1, device_id={"tensor": ten(i)}, device_id_type=MESH)
        return carry

    lax.fori_loop(1, n_dev, greet_dev, 0)
    lax.fori_loop(1, n_ten, greet_ten, 0)

    def rows_of(t, odd, c):
        first = sum(wide[odd] for wide in chunks[:c]) + odd * even_rows
        return pl.ds(pl.multiple_of(t // 2 * pair_rows + first, 16), chunks[c][odd])

    def by_parity(body):
        for odd in range(2):
            pl.when(lax.rem(mine, 2) == odd)(functools.partial(body, odd))

    locals_ = [
        pltpu.make_async_copy(query_ref, q_buf, local_sem.at[0]),
        pltpu.make_async_copy(wk_ref, wk_buf, local_sem.at[1]),
        pltpu.make_async_copy(prefix_ref, prefix_buf, local_sem.at[2]),
        pltpu.make_async_copy(home_ref.at[mine], home_buf, local_sem.at[3]),
        pltpu.make_async_copy(wv_ref, wv_buf, local_sem.at[4]),
    ]
    for copy in locals_:
        copy.start()

    def own_copy(odd, c):
        return pltpu.make_async_copy(
            pool_ref.at[me, rows_of(mine, odd, c)],
            pool_recv[c].at[me, pl.ds(0, chunks[c][odd])],
            local_sem.at[5 + c],
        )

    def block_copy(i, odd, c, source, target):
        return pltpu.make_async_remote_copy(
            src_ref=pool_ref.at[target, rows_of(mine, odd, c)],
            dst_ref=pool_recv[c].at[source, pl.ds(0, chunks[c][odd])],
            send_sem=s_send_sem.at[c, i],
            recv_sem=s_recv_sem.at[c, i],
            device_id={"branch": target},
            device_id_type=MESH,
        )

    pl.semaphore_wait(barrier, n_dev - 1 + n_ten - 1)

    @by_parity
    def _(odd):
        for c in range(n_chunk):

            def send_block(i, carry, c=c):
                block_copy(i, odd, c, me, dev(i)).start()
                return carry

            lax.fori_loop(1, n_dev, send_block, 0)
            own_copy(odd, c).start()

    locals_[0].wait()
    q_flat = q_buf[...].reshape(bs * heads, nope + rope).astype(jnp.float32)
    flat_buf[0, :, pl.ds(0, nope)] = q_flat[:, :nope]
    flat_buf[1, :, pl.ds(0, rope)] = q_flat[:, nope:]
    locals_[1].wait()
    tiles = latent // 128
    for h in range(heads):
        q_head = flat_buf[0, pl.ds(h, bs, stride=heads), :][:, :nope]
        lat_head = jnp.dot(
            q_head.astype(jnp.bfloat16), wk_buf[h], preferred_element_type=jnp.float32
        )
        for j in range(tiles):
            lat_buf[j, pl.ds(h * bs, bs), :] = lat_head[:, j * 128 : (j + 1) * 128]
        lat_buf[tiles, pl.ds(h * bs, bs), :] = flat_buf[1, pl.ds(h, bs, stride=heads), :]
    for b in range(branches):
        for s in range(steps):
            for j in range(tiles + 1):
                wide = 128 if j < tiles else rope
                full_send[b, pl.ds(s * heads, heads), pl.ds(j * 128, wide)] = lat_buf[
                    j, pl.ds(b * steps + s, heads, stride=bs), :
                ][:, :wide].astype(jnp.bfloat16)
    part = width // n_ten
    fresh_send[...] = jnp.zeros_like(fresh_send)
    for b in range(branches):
        fresh_send[b, pl.ds(0, steps), pl.ds(0, part)] = fresh_ref[b]

    def full_copy(i, source, target):
        return pltpu.make_async_remote_copy(
            src_ref=full_send.at[target],
            dst_ref=full_recv.at[source],
            send_sem=q_send_sem.at[i],
            recv_sem=q_recv_sem.at[i],
            device_id={"tensor": target},
            device_id_type=MESH,
        )

    def fresh_copy(i, source, target):
        return pltpu.make_async_remote_copy(
            src_ref=fresh_send.at[target],
            dst_ref=fresh_recv.at[source],
            send_sem=f_send_sem.at[i],
            recv_sem=f_recv_sem.at[i],
            device_id={"tensor": target},
            device_id_type=MESH,
        )

    for i in range(1, n_ten):
        full_copy(i, mine, ten(i)).start()
        fresh_copy(i, mine, ten(i)).start()
    full_recv[mine] = full_send[mine]
    fresh_recv[mine] = fresh_send[mine]
    for i in range(1, n_ten):
        full_copy(i, ten(n_ten - i), mine).wait_recv()
        fresh_copy(i, ten(n_ten - i), mine).wait_recv()

    fresh_all = jnp.zeros((fresh_recv.shape[1], width + fresh_recv.shape[2]), jnp.float32)
    for t in range(n_ten):
        piece = fresh_recv[t].astype(jnp.float32)
        piece = jnp.concatenate([piece, jnp.zeros((piece.shape[0], width), jnp.float32)], 1)
        fresh_all = fresh_all + (pltpu.roll(piece, t * part, 1) if t else piece)
    new_buf[...] = jnp.zeros_like(new_buf)
    new_buf[pl.ds(0, fresh_recv.shape[1]), :] = fresh_all[:, :width].astype(jnp.bfloat16)

    queries = full_recv[...].reshape(all_rows, width)
    length = len_ref[mine]

    def attend(scores, combine):
        peak_old = peak_buf[...]
        peak = jnp.maximum(peak_old, jnp.max(scores, 1, keepdims=True))
        weights = jnp.exp2(scores - peak)
        factor = jnp.exp2(peak_old - peak)
        mass_buf[...] = mass_buf[...] * factor + jnp.sum(weights, 1, keepdims=True)
        peak_buf[...] = peak
        acc_buf[...] = acc_buf[...] * factor + combine(weights.astype(jnp.bfloat16))

    def attend_columns(keys, bound):
        scores = jnp.dot(queries, keys, preferred_element_type=jnp.float32) * scale
        if bound is not None:
            column = lax.broadcasted_iota(jnp.int32, scores.shape, 1)
            scores = jnp.where(column < bound, scores, FLOOR)
        attend(scores, lambda weights: nt_dot(weights, keys[:latent]))

    peak_buf[...] = jnp.full_like(peak_buf, FLOOR)
    mass_buf[...] = jnp.zeros_like(mass_buf)
    acc_buf[...] = jnp.zeros_like(acc_buf)
    locals_[2].wait()

    def prefix_tile(j, carry):
        attend_columns(prefix_buf[:, pl.ds(pl.multiple_of(j * KEY_TILE, KEY_TILE), KEY_TILE)], None)
        return carry

    lax.fori_loop(0, prefix_buf.shape[1] // KEY_TILE, prefix_tile, 0)

    locals_[3].wait()
    attend_columns(home_buf[...], length)
    keys = new_buf[...]
    scores = nt_dot(queries, keys) * scale
    column = lax.broadcasted_iota(jnp.int32, scores.shape, 1)
    row_step = lax.broadcasted_iota(jnp.int32, scores.shape, 0) // heads % steps
    attend(
        jnp.where(column <= row_step, scores, FLOOR),
        lambda weights: jnp.dot(weights, keys[:, :latent], preferred_element_type=jnp.float32),
    )

    def regroup_copy(i, odd, c, source, target):
        return pltpu.make_async_remote_copy(
            src_ref=stage[c].at[target, pl.ds(0, chunks[c][odd])],
            dst_ref=spill.at[rows_of(source, odd, c)],
            send_sem=x_send_sem.at[c, i],
            recv_sem=x_recv_sem.at[c, i],
            device_id={"tensor": target},
            device_id_type=MESH,
        )

    @by_parity
    def _(odd):
        for c in range(n_chunk):

            def wait_block(i, carry, c=c):
                block_copy(i, odd, c, dev(n_dev - i), me).wait_recv()
                return carry

            lax.fori_loop(1, n_dev, wait_block, 0)
            own_copy(odd, c).wait()
            some = pl.ds(0, chunks[c][odd])
            for i in range(1, n_ten):
                target = ten(i)
                for k in range(per_branch):
                    holder = table_ref[k, target] // n_dev
                    stage[c][target, some, pl.ds(k * block, block)] = pool_recv[c][holder, some, :]
                regroup_copy(i, odd, c, mine, target).start()
            for k in range(per_branch):
                holder = table_ref[k, mine] // n_dev
                spill[rows_of(mine, odd, c), pl.ds(k * block, block)] = pool_recv[c][
                    holder, some, :
                ]
        for c in range(n_chunk):
            for i in range(1, n_ten):
                regroup_copy(i, (odd + i) % 2, c, ten(n_ten - i), mine).wait_recv()

    attend_columns(spill[...], length - home)

    lo_send[...] = (acc_buf[...] / mass_buf[...]).astype(jnp.bfloat16).reshape(lo_send.shape)

    def back_copy(i, source, target):
        return pltpu.make_async_remote_copy(
            src_ref=lo_send.at[target],
            dst_ref=lo_recv.at[source],
            send_sem=o_send_sem.at[i],
            recv_sem=o_recv_sem.at[i],
            device_id={"tensor": target},
            device_id_type=MESH,
        )

    for i in range(1, n_ten):
        back_copy(i, mine, ten(i)).start()
    lo_recv[mine] = lo_send[mine]
    locals_[4].wait()
    for i in range(1, n_ten):
        back_copy(i, ten(n_ten - i), mine).wait_recv()
    for j in range(tiles):
        lat_buf[j] = (
            lo_recv[:, :, pl.ds(j * 128, 128)].reshape(branches * rows, 128).astype(jnp.float32)
        )
    for h in range(heads):
        head_rows = jnp.concatenate(
            [lat_buf[j, pl.ds(h, bs, stride=heads), :] for j in range(tiles)], 1
        ).astype(jnp.bfloat16)
        out_buf[pl.ds(h, bs, stride=heads), :] = jnp.dot(
            head_rows, wv_buf[h], preferred_element_type=jnp.float32
        )
    out_ref[...] = out_buf[...].reshape(out_ref.shape).astype(jnp.bfloat16)

    @by_parity
    def _(odd):
        for c in range(n_chunk):

            def sent_block(i, carry, c=c):
                block_copy(i, odd, c, me, dev(i)).wait_send()
                return carry

            lax.fori_loop(1, n_dev, sent_block, 0)
            for i in range(1, n_ten):
                regroup_copy(i, odd, c, mine, ten(i)).wait_send()

    for i in range(1, n_ten):
        full_copy(i, mine, ten(i)).wait_send()
        fresh_copy(i, mine, ten(i)).wait_send()
        back_copy(i, mine, ten(i)).wait_send()


def per_device(
    query,
    absorb_key,
    absorb_value,
    prefix_cache,
    home_cache,
    spill_pool,
    new_latent,
    lengths,
    spill_table,
):
    branches, steps, heads, q_width = query.shape
    nope, latent = absorb_key.shape[1:]
    v_width = absorb_value.shape[2]
    rope = q_width - nope
    width = latent + rope
    home = home_cache.shape[1]
    block = spill_pool.shape[1]
    n_dev = lax.axis_size("branch")
    n_ten = lax.axis_size("tensor")
    per_branch = spill_table.shape[1]
    units = 2 * width // n_ten // 16
    chunks = (((units + 1) // 2 * 16, units // 2 * 16),)
    dims = (
        n_dev, n_ten, branches, steps, heads, nope, rope, latent, home, block, per_branch, chunks
    )
    rows = steps * heads
    bs = branches * steps
    bf16, f32 = jnp.bfloat16, jnp.float32
    hbm = pl.BlockSpec(memory_space=pltpu.HBM)
    smem = pl.BlockSpec(memory_space=pltpu.SMEM)
    vmem = pl.BlockSpec(memory_space=pltpu.VMEM)
    dma = pltpu.SemaphoreType.DMA
    n_chunk = len(chunks)
    out = pl.pallas_call(
        functools.partial(attention_kernel, dims),
        out_shape=jax.ShapeDtypeStruct((bs, heads, v_width), bf16),
        in_specs=[hbm, hbm, hbm, hbm, hbm, hbm, vmem, smem, smem],
        out_specs=vmem,
        scratch_shapes=[
            pltpu.VMEM((bs, heads, q_width), bf16),
            pltpu.VMEM(absorb_key.shape, bf16),
            pltpu.VMEM(absorb_value.shape, bf16),
            pltpu.VMEM(prefix_cache.shape[::-1], bf16),
            pltpu.VMEM((width, home), bf16),
            pltpu.VMEM((128, width), bf16),
            pltpu.VMEM((width, per_branch * block), bf16),
            pltpu.VMEM((2, bs * heads, 128), f32),
            pltpu.VMEM((latent // 128 + 1, bs * heads, 128), f32),
            pltpu.VMEM((branches, rows, width), bf16),
            pltpu.VMEM((n_ten, rows, width), bf16),
            pltpu.VMEM((branches, 16, 128), bf16),
            pltpu.VMEM((n_ten, 16, 128), bf16),
            pltpu.VMEM((n_ten * rows, 1), f32),
            pltpu.VMEM((n_ten * rows, 1), f32),
            pltpu.VMEM((n_ten * rows, latent), f32),
            pltpu.VMEM((n_ten, rows, latent), bf16),
            pltpu.VMEM((branches, rows, latent), bf16),
            pltpu.VMEM((bs * heads, v_width), f32),
            dma((5 + n_chunk,)),
            dma((n_ten,)),
            dma((n_ten,)),
            dma((n_ten,)),
            dma((n_ten,)),
            dma((n_chunk, n_dev)),
            dma((n_chunk, n_dev)),
            dma((n_chunk, n_ten)),
            dma((n_chunk, n_ten)),
            dma((n_ten,)),
            dma((n_ten,)),
        ]
        + [pltpu.VMEM((n_dev, wide[0], block), bf16) for wide in chunks]
        + [pltpu.VMEM((branches, wide[0], per_branch * block), bf16) for wide in chunks],
        compiler_params=pltpu.CompilerParams(
            collective_id=0, has_side_effects=True, vmem_limit_bytes=60 * 1024 * 1024
        ),
    )(
        query.reshape(bs, heads, q_width),
        absorb_key,
        absorb_value,
        prefix_cache.T,
        home_cache.swapaxes(1, 2),
        spill_pool.swapaxes(1, 2),
        new_latent,
        lengths,
        spill_table.T,
    )
    return out.reshape(branches, steps, heads, v_width)


def solution(mesh):
    in_specs = (
        P("branch", None, "tensor", None),
        P("tensor", None, None),
        P("tensor", None, None),
        P(),
        P("branch", None, None),
        P("branch", None, None),
        P("branch", None, "tensor"),
        P("branch"),
        P("branch", None),
    )
    out_specs = P("branch", None, "tensor", None)
    return jax.shard_map(
        per_device, mesh=mesh, in_specs=in_specs, out_specs=out_specs, check_vma=False
    )
```

time: 146 us -> 44.2 us (0.30)
  the two profiles are of different devices: /device:TPU:6 before, /device:TPU:1 now
where the time goes in v1:
time: 44.2 us; the launch traced here: 44.1 us
  Pallas kernels  42.6 us (96%)
  local copies, waits for them, and re-layouts  1.47 us (3%)
    pallas_call x1, Pallas kernels, per_device(): pl.pallas_call(functools.partial(attention_kernel, dims), out_shape=jax.S...  42.6 us
    unnamed x1, local copies, waits for them, and re-layouts  1.47 us

profile of v1, /device:TPU:1, one launch (start us, length us, event | category | flops | bytes accessed | tf_op | source)
XLA Modules:
  0.0 44.1 jit_solution(11403786767034373540)
XLA Ops:
  0.0 42.6 %shard_map.91 = bf16[16,16,128]{2,1,0:T(8,128)(2,1)} custom-call(bf16[16,16,192]{2,1,0:T(8,128)(2,1)} %bitcast.10, bf16[16,128,512]{2,1,0:T(8,128)(2,1)} %wk_ref.1, bf16[16,512,128]{2,1,0:T(8,128)(2,1)} %wv_ref.1, bf16[576,2048]{1,0:T(8,128)(2,1)} %bitcast.7, bf16[8,576,256]{2,1,0:T(8,128)(2,1)} %bitcast.8, bf16[32,576,128]{2,1,0:T(8,128)(2,1)} %bitcast.6, ...), custom_call_target="tpu_custom_call" | custom-call | tf_op jit(solution)/shard_map/pallas_call | solution.py:370
  42.6 1.5 %copy.11 = bf16[8,2,16,128]{3,2,1,0:T(8,128)(2,1)} copy(bf16[8,2,16,128]{3,2,1,0:T(8,128)(2,1)} %bitcast.9) | data formatting | bytes 131072

commit v2 on v1

--- a/solution.py
+++ b/solution.py
@@ -25,10 +25,13 @@
     prefix_ref,
     home_ref,
     pool_ref,
+    fresh_hbm,
+    len_hbm,
+    table_hbm,
+    out_ref,
     fresh_ref,
     len_ref,
     table_ref,
-    out_ref,
     q_buf,
     wk_buf,
     wv_buf,
@@ -108,6 +111,9 @@
         pltpu.make_async_copy(prefix_ref, prefix_buf, local_sem.at[2]),
         pltpu.make_async_copy(home_ref.at[mine], home_buf, local_sem.at[3]),
         pltpu.make_async_copy(wv_ref, wv_buf, local_sem.at[4]),
+        pltpu.make_async_copy(fresh_hbm, fresh_ref, local_sem.at[5]),
+        pltpu.make_async_copy(len_hbm, len_ref, local_sem.at[6]),
+        pltpu.make_async_copy(table_hbm, table_ref, local_sem.at[7]),
     ]
     for copy in locals_:
         copy.start()
@@ -116,31 +122,22 @@
         return pltpu.make_async_copy(
             pool_ref.at[me, rows_of(mine, odd, c)],
             pool_recv[c].at[me, pl.ds(0, chunks[c][odd])],
-            local_sem.at[5 + c],
-        )
-
-    def block_copy(i, odd, c, source, target):
+            local_sem.at[8 + c],
+        )
+
+    def all_blocks(odd, c, sem):
+        landed = pool_recv[c].at[pl.ds(0, n_dev - 1), pl.ds(0, chunks[c][odd])]
+        return pltpu.make_async_copy(landed, landed, sem.at[c])
+
+    def block_copy(odd, c, source, target):
         return pltpu.make_async_remote_copy(
             src_ref=pool_ref.at[target, rows_of(mine, odd, c)],
             dst_ref=pool_recv[c].at[source, pl.ds(0, chunks[c][odd])],
-            send_sem=s_send_sem.at[c, i],
-            recv_sem=s_recv_sem.at[c, i],
+            send_sem=s_send_sem.at[c],
+            recv_sem=s_recv_sem.at[c],
             device_id={"branch": target},
             device_id_type=MESH,
         )
-
-    pl.semaphore_wait(barrier, n_dev - 1 + n_ten - 1)
-
-    @by_parity
-    def _(odd):
-        for c in range(n_chunk):
-
-            def send_block(i, carry, c=c):
-                block_copy(i, odd, c, me, dev(i)).start()
-                return carry
-
-            lax.fori_loop(1, n_dev, send_block, 0)
-            own_copy(odd, c).start()
 
     locals_[0].wait()
     q_flat = q_buf[...].reshape(bs * heads, nope + rope).astype(jnp.float32)
@@ -165,8 +162,11 @@
                 ][:, :wide].astype(jnp.bfloat16)
     part = width // n_ten
     fresh_send[...] = jnp.zeros_like(fresh_send)
+    locals_[5].wait()
     for b in range(branches):
         fresh_send[b, pl.ds(0, steps), pl.ds(0, part)] = fresh_ref[b]
+
+    pl.semaphore_wait(barrier, n_dev - 1 + n_ten - 1)
 
     def full_copy(i, source, target):
         return pltpu.make_async_remote_copy(
@@ -188,11 +188,26 @@
             device_id_type=MESH,
         )
 
+    def send_blocks(chosen):
+        @by_parity
+        def _(odd):
+            for c in chosen:
+
+                def send_block(i, carry, c=c):
+                    block_copy(odd, c, me, dev(i)).start()
+                    return carry
+
+                lax.fori_loop(1, n_dev, send_block, 0)
+                own_copy(odd, c).start()
+
+    send_blocks(range(1))
     for i in range(1, n_ten):
         full_copy(i, mine, ten(i)).start()
         fresh_copy(i, mine, ten(i)).start()
     full_recv[mine] = full_send[mine]
     fresh_recv[mine] = fresh_send[mine]
+    send_blocks(range(1, n_chunk))
+
     for i in range(1, n_ten):
         full_copy(i, ten(n_ten - i), mine).wait_recv()
         fresh_copy(i, ten(n_ten - i), mine).wait_recv()
@@ -206,6 +221,8 @@
     new_buf[pl.ds(0, fresh_recv.shape[1]), :] = fresh_all[:, :width].astype(jnp.bfloat16)
 
     queries = full_recv[...].reshape(all_rows, width)
+    locals_[6].wait()
+    locals_[7].wait()
     length = len_ref[mine]
 
     def attend(scores, combine):
@@ -234,6 +251,38 @@
         return carry
 
     lax.fori_loop(0, prefix_buf.shape[1] // KEY_TILE, prefix_tile, 0)
+
+    def regroup_copy(i, odd, c, source, target):
+        return pltpu.make_async_remote_copy(
+            src_ref=stage[c].at[target, pl.ds(0, chunks[c][odd])],
+            dst_ref=spill.at[rows_of(source, odd, c)],
+            send_sem=x_send_sem.at[c, i],
+            recv_sem=x_recv_sem.at[c, i],
+            device_id={"tensor": target},
+            device_id_type=MESH,
+        )
+
+    def regroup(chosen):
+        @by_parity
+        def _(odd):
+            for c in chosen:
+
+                all_blocks(odd, c, s_recv_sem).wait()
+                own_copy(odd, c).wait()
+                some = pl.ds(0, chunks[c][odd])
+                for i in range(1, n_ten):
+                    target = ten(i)
+                    for k in range(per_branch):
+                        holder = table_ref[k, target] // n_dev
+                        stage[c][target, some, pl.ds(k * block, block)] = pool_recv[c][holder, some, :]
+                    regroup_copy(i, odd, c, mine, target).start()
+                for k in range(per_branch):
+                    holder = table_ref[k, mine] // n_dev
+                    spill[rows_of(mine, odd, c), pl.ds(k * block, block)] = pool_recv[c][
+                        holder, some, :
+                    ]
+
+    regroup(range(n_chunk - 1))
 
     locals_[3].wait()
     attend_columns(home_buf[...], length)
@@ -246,62 +295,49 @@
         lambda weights: jnp.dot(weights, keys[:, :latent], preferred_element_type=jnp.float32),
     )
 
-    def regroup_copy(i, odd, c, source, target):
-        return pltpu.make_async_remote_copy(
-            src_ref=stage[c].at[target, pl.ds(0, chunks[c][odd])],
-            dst_ref=spill.at[rows_of(source, odd, c)],
-            send_sem=x_send_sem.at[c, i],
-            recv_sem=x_recv_sem.at[c, i],
-            device_id={"tensor": target},
-            device_id_type=MESH,
-        )
+    regroup(range(n_chunk - 1, n_chunk))
 
     @by_parity
     def _(odd):
         for c in range(n_chunk):
-
-            def wait_block(i, carry, c=c):
-                block_copy(i, odd, c, dev(n_dev - i), me).wait_recv()
-                return carry
-
-            lax.fori_loop(1, n_dev, wait_block, 0)
-            own_copy(odd, c).wait()
-            some = pl.ds(0, chunks[c][odd])
-            for i in range(1, n_ten):
-                target = ten(i)
-                for k in range(per_branch):
-                    holder = table_ref[k, target] // n_dev
-                    stage[c][target, some, pl.ds(k * block, block)] = pool_recv[c][holder, some, :]
-                regroup_copy(i, odd, c, mine, target).start()
-            for k in range(per_branch):
-                holder = table_ref[k, mine] // n_dev
-                spill[rows_of(mine, odd, c), pl.ds(k * block, block)] = pool_recv[c][
-                    holder, some, :
-                ]
-        for c in range(n_chunk):
             for i in range(1, n_ten):
                 regroup_copy(i, (odd + i) % 2, c, ten(n_ten - i), mine).wait_recv()
 
     attend_columns(spill[...], length - home)
 
-    lo_send[...] = (acc_buf[...] / mass_buf[...]).astype(jnp.bfloat16).reshape(lo_send.shape)
-
-    def back_copy(i, source, target):
+    lo_send[...] = (acc_buf[...] * (1.0 / mass_buf[...])).astype(jnp.bfloat16).reshape(lo_send.shape)
+
+    def all_back(sem):
+        landed = lo_recv.at[pl.ds(0, n_ten - 1)]
+        return pltpu.make_async_copy(landed, landed, sem)
+
+    def back_copy(source, target):
         return pltpu.make_async_remote_copy(
             src_ref=lo_send.at[target],
             dst_ref=lo_recv.at[source],
-            send_sem=o_send_sem.at[i],
-            recv_sem=o_recv_sem.at[i],
+            send_sem=o_send_sem,
+            recv_sem=o_recv_sem,
             device_id={"tensor": target},
             device_id_type=MESH,
         )
 
     for i in range(1, n_ten):
-        back_copy(i, mine, ten(i)).start()
+        back_copy(mine, ten(i)).start()
     lo_recv[mine] = lo_send[mine]
+    @by_parity
+    def _(odd):
+        for c in range(n_chunk):
+
+            all_blocks(odd, c, s_send_sem).wait()
+            for i in range(1, n_ten):
+                regroup_copy(i, odd, c, mine, ten(i)).wait_send()
+
+    for i in range(1, n_ten):
+        full_copy(i, mine, ten(i)).wait_send()
+        fresh_copy(i, mine, ten(i)).wait_send()
+
     locals_[4].wait()
-    for i in range(1, n_ten):
-        back_copy(i, ten(n_ten - i), mine).wait_recv()
+    all_back(o_recv_sem).wait()
     for j in range(tiles):
         lat_buf[j] = (
             lo_recv[:, :, pl.ds(j * 128, 128)].reshape(branches * rows, 128).astype(jnp.float32)
@@ -315,22 +351,7 @@
         )
     out_ref[...] = out_buf[...].reshape(out_ref.shape).astype(jnp.bfloat16)
 
-    @by_parity
-    def _(odd):
-        for c in range(n_chunk):
-
-            def sent_block(i, carry, c=c):
-                block_copy(i, odd, c, me, dev(i)).wait_send()
-                return carry
-
-            lax.fori_loop(1, n_dev, sent_block, 0)
-            for i in range(1, n_ten):
-                regroup_copy(i, odd, c, mine, ten(i)).wait_send()
-
-    for i in range(1, n_ten):
-        full_copy(i, mine, ten(i)).wait_send()
-        fresh_copy(i, mine, ten(i)).wait_send()
-        back_copy(i, mine, ten(i)).wait_send()
+    all_back(o_send_sem).wait()
 
 
 def per_device(
@@ -354,8 +375,7 @@
     n_dev = lax.axis_size("branch")
     n_ten = lax.axis_size("tensor")
     per_branch = spill_table.shape[1]
-    units = 2 * width // n_ten // 16
-    chunks = (((units + 1) // 2 * 16, units // 2 * 16),)
+    chunks = ((48, 48), (32, 16))
     dims = (
         n_dev, n_ten, branches, steps, heads, nope, rope, latent, home, block, per_branch, chunks
     )
@@ -363,16 +383,18 @@
     bs = branches * steps
     bf16, f32 = jnp.bfloat16, jnp.float32
     hbm = pl.BlockSpec(memory_space=pltpu.HBM)
-    smem = pl.BlockSpec(memory_space=pltpu.SMEM)
     vmem = pl.BlockSpec(memory_space=pltpu.VMEM)
     dma = pltpu.SemaphoreType.DMA
     n_chunk = len(chunks)
     out = pl.pallas_call(
         functools.partial(attention_kernel, dims),
-        out_shape=jax.ShapeDtypeStruct((bs, heads, v_width), bf16),
-        in_specs=[hbm, hbm, hbm, hbm, hbm, hbm, vmem, smem, smem],
+        out_shape=pltpu.VMEM((bs, heads, v_width), bf16),
+        in_specs=[hbm] * 9,
         out_specs=vmem,
         scratch_shapes=[
+            pltpu.VMEM(new_latent.shape, bf16),
+            pltpu.SMEM(lengths.shape, jnp.int32),
+            pltpu.SMEM(spill_table.shape[::-1], jnp.int32),
             pltpu.VMEM((bs, heads, q_width), bf16),
             pltpu.VMEM(absorb_key.shape, bf16),
             pltpu.VMEM(absorb_value.shape, bf16),
@@ -392,17 +414,17 @@
             pltpu.VMEM((n_ten, rows, latent), bf16),
             pltpu.VMEM((branches, rows, latent), bf16),
             pltpu.VMEM((bs * heads, v_width), f32),
-            dma((5 + n_chunk,)),
+            dma((8 + n_chunk,)),
             dma((n_ten,)),
             dma((n_ten,)),
             dma((n_ten,)),
             dma((n_ten,)),
-            dma((n_chunk, n_dev)),
-            dma((n_chunk, n_dev)),
+            dma((n_chunk,)),
+            dma((n_chunk,)),
             dma((n_chunk, n_ten)),
             dma((n_chunk, n_ten)),
-            dma((n_ten,)),
-            dma((n_ten,)),
+            dma,
+            dma,
         ]
         + [pltpu.VMEM((n_dev, wide[0], block), bf16) for wide in chunks]
         + [pltpu.VMEM((branches, wide[0], per_branch * block), bf16) for wide in chunks],

time: 44.2 us -> 38.9 us (0.88)
  Pallas kernels: 42.6 us -> 38.2 us
  local copies, waits for them, and re-layouts: 1.47 us -> 0.63 us
    pallas_call x1, Pallas kernels: 42.6 us -> 38.2 us  [per_device(): pl.pallas_call(functools.partial(attention_kernel, dims), out_shape=pltpu...]
    unnamed x1, local copies, waits for them, and re-layouts: 1.47 us -> 0.63 us
where the time goes in v2:
time: 38.9 us
  Pallas kernels  38.2 us (98%)
  local copies, waits for them, and re-layouts  0.63 us (2%)
    pallas_call x1, Pallas kernels, per_device(): pl.pallas_call(functools.partial(attention_kernel, dims), out_shape=pltpu...  38.2 us

profile of v2, /device:TPU:1, one launch (start us, length us, event | category | flops | bytes accessed | tf_op | source)
XLA Modules:
  0.0 38.9 jit_solution(11179997591312301366)
XLA Ops:
  0.0 38.2 %shard_map.91 = bf16[16,16,128]{2,1,0:T(8,128)(2,1)S(1)} custom-call(bf16[16,16,192]{2,1,0:T(8,128)(2,1)} %bitcast.10, bf16[16,128,512]{2,1,0:T(8,128)(2,1)} %wk_ref.1, bf16[16,512,128]{2,1,0:T(8,128)(2,1)} %wv_ref.1, bf16[576,2048]{1,0:T(8,128)(2,1)} %bitcast.8, bf16[8,576,256]{2,1,0:T(8,128)(2,1)} %bitcast.9, bf16[32,576,128]{2,1,0:T(8,128)(2,1)} %bitcast.7, ...), custom_call_target="tpu_custom_call" | custom-call | tf_op jit(solution)/shard_map/pallas_call | solution.py:389
  38.2 0.6 %copy.11 = bf16[8,2,16,128]{3,2,1,0:T(8,128)(2,1)} copy(bf16[8,2,16,128]{3,2,1,0:T(8,128)(2,1)S(1)} %bitcast.6) | data formatting | bytes 131072

commit v3 on v2

--- a/solution.py
+++ b/solution.py
@@ -11,6 +11,7 @@
 MESH = pl.DeviceIdType.MESH
 FLOOR = -1e30
 KEY_TILE = 512
+DEPTH = 8
 
 
 def nt_dot(a, b):
@@ -70,8 +71,7 @@
     bs = branches * steps
     all_rows = n_ten * rows
     n_chunk = len(chunks)
-    pair_rows = 2 * width // n_ten
-    even_rows = sum(wide[0] for wide in chunks)
+    starts = [sum(sum(wide) for wide in chunks[:c]) * n_ten // 2 for c in range(n_chunk + 1)]
     pool_recv = chunk_bufs[:n_chunk]
     stage = chunk_bufs[n_chunk:]
     me = lax.axis_index("branch")
@@ -84,6 +84,8 @@
     def ten(i):
         return lax.rem(mine + i, n_ten)
 
+    far_first = sorted(range(1, n_ten), key=lambda i: (abs(n_ten // 2 - i), -i))
+
     barrier = pltpu.get_barrier_semaphore()
 
     def greet_dev(i, carry):
@@ -94,12 +96,17 @@
         pl.semaphore_signal(barrier, inc=1, device_id={"tensor": ten(i)}, device_id_type=MESH)
         return carry
 
-    lax.fori_loop(1, n_dev, greet_dev, 0)
+    def hops(i):
+        across, along = divmod(i, DEPTH)
+        return min(across, n_dev // DEPTH - across) + min(along, DEPTH - along)
+
+    for i in sorted(range(1, n_dev), key=hops, reverse=True):
+        greet_dev(i, 0)
     lax.fori_loop(1, n_ten, greet_ten, 0)
 
     def rows_of(t, odd, c):
-        first = sum(wide[odd] for wide in chunks[:c]) + odd * even_rows
-        return pl.ds(pl.multiple_of(t // 2 * pair_rows + first, 16), chunks[c][odd])
+        first = starts[c] + odd * chunks[c][0]
+        return pl.ds(pl.multiple_of(t // 2 * sum(chunks[c]) + first, 16), chunks[c][odd])
 
     def by_parity(body):
         for odd in range(2):
@@ -201,7 +208,7 @@
                 own_copy(odd, c).start()
 
     send_blocks(range(1))
-    for i in range(1, n_ten):
+    for i in far_first:
         full_copy(i, mine, ten(i)).start()
         fresh_copy(i, mine, ten(i)).start()
     full_recv[mine] = full_send[mine]
@@ -270,7 +277,7 @@
                 all_blocks(odd, c, s_recv_sem).wait()
                 own_copy(odd, c).wait()
                 some = pl.ds(0, chunks[c][odd])
-                for i in range(1, n_ten):
+                for i in far_first:
                     target = ten(i)
                     for k in range(per_branch):
                         holder = table_ref[k, target] // n_dev
@@ -297,15 +304,28 @@
 
     regroup(range(n_chunk - 1, n_chunk))
 
-    @by_parity
-    def _(odd):
-        for c in range(n_chunk):
+    scores = 0.0
+    for c in range(n_chunk):
+
+        @by_parity
+        def _(odd, c=c):
             for i in range(1, n_ten):
                 regroup_copy(i, (odd + i) % 2, c, ten(n_ten - i), mine).wait_recv()
 
-    attend_columns(spill[...], length - home)
-
-    lo_send[...] = (acc_buf[...] * (1.0 / mass_buf[...])).astype(jnp.bfloat16).reshape(lo_send.shape)
+        span = slice(starts[c], starts[c + 1])
+        scores += jnp.dot(queries[:, span], spill[span, :], preferred_element_type=jnp.float32)
+
+    column = lax.broadcasted_iota(jnp.int32, scores.shape, 1)
+    scores = jnp.where(column < length - home, scores * scale, FLOOR)
+    peak_old = peak_buf[...]
+    peak = jnp.maximum(peak_old, jnp.max(scores, 1, keepdims=True))
+    weights = jnp.exp2(scores - peak)
+    factor = jnp.exp2(peak_old - peak)
+    share = 1.0 / (mass_buf[...] * factor + jnp.sum(weights, 1, keepdims=True))
+    last = nt_dot(weights.astype(jnp.bfloat16), spill[pl.ds(0, latent), :])
+    lo_send[...] = (
+        (acc_buf[...] * (factor * share) + last * share).astype(jnp.bfloat16).reshape(lo_send.shape)
+    )
 
     def all_back(sem):
         landed = lo_recv.at[pl.ds(0, n_ten - 1)]
@@ -321,7 +341,7 @@
             device_id_type=MESH,
         )
 
-    for i in range(1, n_ten):
+    for i in far_first:
         back_copy(mine, ten(i)).start()
     lo_recv[mine] = lo_send[mine]
     @by_parity

time: 38.9 us -> 38 us (0.977)
  Pallas kernels: 38.2 us -> 37.3 us
    pallas_call x1, Pallas kernels: 38.2 us -> 37.3 us  [per_device(): pl.pallas_call(functools.partial(attention_kernel, dims), out_shape=pltpu...]
where the time goes in v3:
time: 38 us; the launch traced here: 37.9 us
  Pallas kernels  37.3 us (98%)
  local copies, waits for them, and re-layouts  0.63 us (2%)
    pallas_call x1, Pallas kernels, per_device(): pl.pallas_call(functools.partial(attention_kernel, dims), out_shape=pltpu...  37.3 us

profile of v3, /device:TPU:1, one launch (start us, length us, event | category | flops | bytes accessed | tf_op | source)
XLA Modules:
  0.0 37.9 jit_solution(3644928370832966564)
XLA Ops:
  0.0 37.3 %shard_map.91 = bf16[16,16,128]{2,1,0:T(8,128)(2,1)S(1)} custom-call(bf16[16,16,192]{2,1,0:T(8,128)(2,1)} %bitcast.10, bf16[16,128,512]{2,1,0:T(8,128)(2,1)} %wk_ref.1, bf16[16,512,128]{2,1,0:T(8,128)(2,1)} %wv_ref.1, bf16[576,2048]{1,0:T(8,128)(2,1)} %bitcast.8, bf16[8,576,256]{2,1,0:T(8,128)(2,1)} %bitcast.9, bf16[32,576,128]{2,1,0:T(8,128)(2,1)} %bitcast.7, ...), custom_call_target="tpu_custom_call" | custom-call | tf_op jit(solution)/shard_map/pallas_call | solution.py:409
  37.3 0.6 %copy.11 = bf16[8,2,16,128]{3,2,1,0:T(8,128)(2,1)} copy(bf16[8,2,16,128]{3,2,1,0:T(8,128)(2,1)S(1)} %bitcast.6) | data formatting | bytes 131072

commit v4 on v3

--- a/solution.py
+++ b/solution.py
@@ -269,6 +269,8 @@
             device_id_type=MESH,
         )
 
+    holders = [[table_ref[k, ten(i)] // n_dev for k in range(per_branch)] for i in range(n_ten)]
+
     def regroup(chosen):
         @by_parity
         def _(odd):
@@ -279,12 +281,10 @@
                 some = pl.ds(0, chunks[c][odd])
                 for i in far_first:
                     target = ten(i)
-                    for k in range(per_branch):
-                        holder = table_ref[k, target] // n_dev
+                    for k, holder in enumerate(holders[i]):
                         stage[c][target, some, pl.ds(k * block, block)] = pool_recv[c][holder, some, :]
                     regroup_copy(i, odd, c, mine, target).start()
-                for k in range(per_branch):
-                    holder = table_ref[k, mine] // n_dev
+                for k, holder in enumerate(holders[0]):
                     spill[rows_of(mine, odd, c), pl.ds(k * block, block)] = pool_recv[c][
                         holder, some, :
                     ]

time: 38 us -> 37.9 us (level)
  no operation moved by 1% of the time
where the time goes in v4:
time: 37.9 us
  Pallas kernels  37.2 us (98%)
  local copies, waits for them, and re-layouts  0.63 us (2%)
    pallas_call x1, Pallas kernels, per_device(): pl.pallas_call(functools.partial(attention_kernel, dims), out_shape=pltpu...  37.2 us

profile of v4, /device:TPU:1, one launch (start us, length us, event | category | flops | bytes accessed | tf_op | source)
XLA Modules:
  0.0 37.9 jit_solution(3687333185619473557)
XLA Ops:
  0.0 37.2 %shard_map.91 = bf16[16,16,128]{2,1,0:T(8,128)(2,1)S(1)} custom-call(bf16[16,16,192]{2,1,0:T(8,128)(2,1)} %bitcast.10, bf16[16,128,512]{2,1,0:T(8,128)(2,1)} %wk_ref.1, bf16[16,512,128]{2,1,0:T(8,128)(2,1)} %wv_ref.1, bf16[576,2048]{1,0:T(8,128)(2,1)} %bitcast.8, bf16[8,576,256]{2,1,0:T(8,128)(2,1)} %bitcast.9, bf16[32,576,128]{2,1,0:T(8,128)(2,1)} %bitcast.7, ...), custom_call_target="tpu_custom_call" | custom-call | tf_op jit(solution)/shard_map/pallas_call | solution.py:409
  37.2 0.6 %copy.11 = bf16[8,2,16,128]{3,2,1,0:T(8,128)(2,1)} copy(bf16[8,2,16,128]{3,2,1,0:T(8,128)(2,1)S(1)} %bitcast.6) | data formatting | bytes 131072
